TPU v7x, 32 devices: a whole 2x2x4 slice. The times are simulated.
32 devices in a mesh: batch: 16 (over z, y, x), mp: 2 (over core).
Axes of the slice: x: 2, y: 2, z: 4, core: 2. Of those that a mesh axis runs over, the one named last changes fastest.
Arguments:
- features: bfloat16 [131072, 512], P('batch'), may hold values from -67 to 67, as said below
- validity: int32 [131072], P('batch'), may hold values from 0 to 1, as said below
- labels: int32 [131072, 2], P('batch'), may hold values from 0 to 1
- expert_in: float32 [6, 512, 256], P(None, None, 'mp'), may hold values from -0.25 to 0.25
- expert_in_bias: float32 [6, 256], P(None, 'mp'), may hold values from -2 to 2
- norm_gain: float32 [6, 256], P(None, 'mp'), may hold values from 0.25 to 1.75
- norm_bias: float32 [6, 256], P(None, 'mp'), may hold values from -2 to 2
- expert_out: float32 [6, 256, 256], P(None, 'mp'), may hold values from -0.375 to 0.375
- expert_out_bias: float32 [6, 256], replicated, may hold values from -2 to 2
- gate_weight: float32 [2, 512, 4], replicated, may hold values from -0.25 to 0.25
- gate_bias: float32 [2, 4], replicated, may hold values from -0.1 to 0.1
- tower_first: float32 [2, 256, 128], replicated, may hold values from -0.375 to 0.375
- tower_first_bias: float32 [2, 128], replicated, may hold values from -2 to 2
- tower_second: float32 [2, 128, 64], replicated, may hold values from -0.5 to 0.5
- tower_second_bias: float32 [2, 64], replicated, may hold values from -2 to 2
- tower_last: float32 [2, 64], replicated, may hold values from -0.75 to 0.75
- tower_last_bias: float32 [2], replicated, may hold values from -2 to 2
Outputs:
- predictions: float32 [131072, 2], P('batch')
- features_grad: float32 [131072, 512], P('batch', 'mp')
- grad_expert_in: float32 [6, 512, 256], P(None, None, 'mp')
- grad_expert_in_bias: float32 [6, 256], P(None, 'mp')
- grad_norm_gain: float32 [6, 256], P(None, 'mp')
- grad_norm_bias: float32 [6, 256], P(None, 'mp')
- grad_expert_out: float32 [6, 256, 256], P(None, 'mp')
- grad_expert_out_bias: float32 [6, 256], replicated
- grad_gate_weight: float32 [2, 512, 4], replicated
- grad_gate_bias: float32 [2, 4], replicated
- grad_tower_first: float32 [2, 256, 128], replicated
- grad_tower_first_bias: float32 [2, 128], replicated
- grad_tower_second: float32 [2, 128, 64], replicated
- grad_tower_second_bias: float32 [2, 64], replicated
- grad_tower_last: float32 [2, 64], replicated
- grad_tower_last_bias: float32 [2], replicated
Inputs may be any that keep to these rules, and one draw needn't show every extreme that they name: The features have a per-feature offset and scale. `validity`: each index of batch holds between 2048 and 8192 valid events; low indices tend to hold fewer than high ones, but neighbouring indices may be in either order.
All inputs are finite; a program needn't handle non-finite values.
Results may differ from a plain program's by a relative error of at most 0.0075.
Values may be sent and summed in bfloat16 or wider, within the bound.
A program may use at most 320 MiB of HBM per device.

v0:
```python
import functools

import jax
import jax.numpy as jnp
from jax import lax
from jax.experimental import pallas as pl
from jax.experimental.pallas import tpu as pltpu
from jax.sharding import PartitionSpec as P

MESH = pl.DeviceIdType.MESH
F32 = jnp.float32
BF16 = jnp.bfloat16
EPS = 1e-05
TASK_EXPERTS = ((0, 1, 4, 5), (2, 3, 4, 5))
E = 6
H = 256
D = 512
TF = 256
TB = 512
SB = 256
CH = 32
VR = 72
HE = H + 16
WIDTHS = (256,) * E + (384,) * 3
NC = len(WIDTHS)
TOWERS = E


def levels_of(count):
    levels, stride = [], 1
    while stride < count:
        radix = 4 if (count // stride) % 4 == 0 else count // stride
        levels.append((stride, radix))
        stride *= radix
    return levels


def plan_of(count):
    plan, rows = [], H
    for stride, radix in levels_of(count):
        split = rows % radix == 0 and (rows // radix) % 16 == 0
        plan.append((stride, radix, rows, rows // radix if split else rows))
        rows = plan[-1][3]
    return plan


def nn(a, b):
    return lax.dot_general(a, b, (((1,), (0,)), ((), ())), preferred_element_type=F32)


def nt(a, b):
    return lax.dot_general(a, b, (((1,), (1,)), ((), ())), preferred_element_type=F32)


def column(row):
    return jnp.broadcast_to(row, (128, 128)).T


def wide(table, width):
    return jnp.concatenate([table] * (width // 128), axis=1)


def fold8(value):
    total = value[0:8]
    for start in range(8, value.shape[0], 8):
        total = total + value[start : start + 8]
    return total


def fold_lanes(value):
    total = value[:, 0:128]
    for start in range(128, value.shape[1], 128):
        total = total + value[:, start : start + 128]
    return total


def lane_sums(partial):
    rows = [
        jnp.sum(partial[at : at + 128].T, axis=0, keepdims=True)
        for at in range(0, partial.shape[0], 128)
    ]
    return jnp.concatenate(rows, axis=1)


def merge_stats(items):
    count = items[0][2:3]
    total = items[0][0:1]
    for item in items[1:]:
        count = count + item[2:3]
        total = total + item[0:1]
    mean = total / jnp.maximum(count, 1.0)
    square = jnp.zeros_like(total)
    for item in items:
        shift = item[0:1] / jnp.maximum(item[2:3], 1.0) - mean
        square = square + item[1:2] + item[2:3] * shift * shift
    return total, square, count


def main_kernel(
    plan, rows_core,
    x_hbm, v_ref, y_ref, win_hbm, wout_hbm, bin_ref, gain_ref, nb_ref, bout_ref, gate_ref, gb_ref,
    w1_ref, b1_ref, w2_ref, b2_ref, wl_ref, bl_ref,
    d_hbm, pred_hbm, gout_hbm, vout_ref, stat_ref, wb_hbm,
    xbuf, zbuf, sbuf, dobuf, rbuf, dlogbuf, predbuf,
    wf, gback, wot, pk, g2t, b2t,
    w1t, w1n, w2f, w2b, b1t, b2tt, wlt, gbt,
    abufs, hbufs, logit_bufs, mixb, u1b, dmix,
    acc_out, acc_gate, acc_first, acc_second,
    acc_dlog, acc_lb, acc_last, acc_b2, acc_b1, s2row,
    bias_snd, bias_rcv,
    st_near, st_lv, v_mp, v_lv, sends, sends_low, mprecv, lvrecv,
    sem_x, sem_w, sem_st, sem_v, sem_s, sem_r, sem_l, sem_d, sem_f,
):
    R = rows_core
    abuf = abufs[0]
    acc_in = (abuf.at[0:H, :], abuf.at[H : 2 * H, :])
    hkeep = (abuf.at[2 * H : 3 * H, :], abuf.at[3 * H : 4 * H, :])
    acc_u = (
        abuf.at[4 * H : 5 * H, 0:128], abuf.at[4 * H : 5 * H, 128:256], abuf.at[5 * H : 6 * H, 0:128]
    )
    n_levels = len(plan)
    b = lax.axis_index("batch")
    mp = lax.axis_index("mp")
    other = 1 - mp
    digits = [lax.rem(lax.div(b, stride), radix) for stride, radix, _, _ in plan]

    def peer(level, step):
        stride, radix = plan[level][:2]
        to = lax.rem(digits[level] + step, radix)
        return (b + (to - digits[level]) * stride, mp)

    def send(src, dst, ssem, rsem, to):
        copy = pltpu.make_async_remote_copy(
            src_ref=src, dst_ref=dst, send_sem=ssem, recv_sem=rsem,
            device_id=to, device_id_type=MESH,
        )
        copy.start()
        return copy

    n_x = 8
    xr = R // n_x
    x_copies = []
    for k in range(n_x):
        copy = pltpu.make_async_copy(
            x_hbm.at[pl.ds(pl.multiple_of(mp * R + k * xr, 16), xr), :],
            xbuf.at[pl.ds(k * xr, xr), :],
            sem_x.at[k],
        )
        copy.start()
        x_copies.append(copy)

    f_copies = []
    for e in range(E):
        for k in range(2):
            f_copies.append(
                pltpu.make_async_copy(
                    win_hbm.at[e, k * H : (k + 1) * H, :],
                    abuf.at[e * H : (e + 1) * H, k * 128 : (k + 1) * 128],
                    sem_f.at[2 * e + k],
                )
            )
        f_copies.append(
            pltpu.make_async_copy(
                wout_hbm.at[e], acc_out.at[e * 128 : (e + 1) * 128, :], sem_f.at[2 * E + e]
            )
        )
    for copy in f_copies:
        copy.start()

    barrier = pltpu.get_barrier_semaphore()
    near = [(step, m) for step in range(plan[0][1]) for m in range(2) if step or m]

    def near_peer(step, m):
        return (peer(0, step)[0], other if m else mp)

    greets = [near_peer(step, m) for step, m in near]
    for level in range(1, n_levels):
        greets += [peer(level, step) for step in range(1, plan[level][1])]
    for to in greets:
        pl.semaphore_signal(barrier, inc=1, device_id=to, device_id_type=MESH)

    v_row = v_ref[:, pl.ds(pl.multiple_of(mp * R, 128), R)].astype(F32)
    count = jnp.sum(v_row, axis=1, keepdims=True)
    total = jnp.zeros((16, D), F32)
    for k in range(n_x):
        x_copies[k].wait()
        v16 = jnp.broadcast_to(v_row[:, k * xr : (k + 1) * xr], (16, xr)).astype(BF16)
        total = total + nn(v16, xbuf[pl.ds(k * xr, xr), :])
    mean = total[0:1] / jnp.maximum(count, 1.0)

    def square_step(k, total):
        for part in range(2):
            r0 = pl.multiple_of(k * 512 + part * 256, 256)
            off = xbuf[pl.ds(r0, 256), :].astype(F32) - mean
            v16 = v_ref[:, pl.ds(pl.multiple_of(mp * R + r0, 128), 256)]
            v16 = jnp.broadcast_to(v16.astype(F32), (16, 256)).astype(BF16)
            total = total + nn(v16, (off * off).astype(BF16))
        return total

    square = lax.fori_loop(0, R // 512, square_step, jnp.zeros((16, D), F32))
    pl.semaphore_wait(barrier, len(greets))
    me = digits[0] * 2 + mp
    st_near[me] = jnp.concatenate(
        [total[0:1], square[0:1], jnp.broadcast_to(count, (1, D)), jnp.zeros((5, D), F32)], axis=0
    )
    st_copies = [
        send(st_near.at[me], st_near.at[me], sem_st.at[2 * k], sem_st.at[2 * k + 1], near_peer(*near[k]))
        for k in range(len(near))
    ]

    win_snd = dobuf.at[0:D, 0 : E * 128]
    win_rcv = dobuf.at[0:D, 1024 : 1024 + E * 128]
    wout_snd = dobuf.at[D : D + 128, 0 : E * H]
    wout_rcv = dobuf.at[D : D + 128, 2048 : 2048 + E * H]
    for copy in f_copies:
        copy.wait()
    for e in range(E):
        for k in range(2):
            win_snd[k * H : (k + 1) * H, e * 128 : (e + 1) * 128] = abuf[
                e * H : (e + 1) * H, k * 128 : (k + 1) * 128
            ].astype(BF16)
        wout_snd[:, e * H : (e + 1) * H] = acc_out[e * 128 : (e + 1) * 128, :].astype(BF16)
    bias_snd[0:E] = bin_ref[...]
    bias_snd[8 : 8 + E] = gain_ref[...]
    bias_snd[16 : 16 + E] = nb_ref[...]
    w_copies = [
        send(win_snd, win_rcv, sem_w.at[0], sem_w.at[1], (b, other)),
        send(wout_snd, wout_rcv, sem_w.at[2], sem_w.at[3], (b, other)),
        send(bias_snd, bias_rcv, sem_w.at[4], sem_w.at[5], (b, other)),
    ]

    for t in range(2):
        w1n[t] = w1_ref[t].astype(BF16)
        w1t[t] = (w1_ref[t].T * 0.5).astype(BF16)
        b1t[t * 128 : (t + 1) * 128] = column(b1_ref[t : t + 1, :]) * 0.5
    zero64 = jnp.zeros((64, 128), F32)
    zero128 = jnp.zeros((128, 64), F32)
    w2f[0:64] = (jnp.concatenate([w2_ref[0], zero64], axis=1) * 0.5).astype(BF16)
    w2f[64:128] = (jnp.concatenate([zero64, w2_ref[1]], axis=1) * 0.5).astype(BF16)
    w2b[0:128] = (jnp.concatenate([w2_ref[0].T, zero128], axis=1) * 0.5).astype(BF16)
    w2b[128:256] = (jnp.concatenate([zero128, w2_ref[1].T], axis=1) * 0.5).astype(BF16)
    b2tt[...] = column(jnp.concatenate([b2_ref[0:1, :], b2_ref[1:2, :]], axis=1)) * 0.5
    wlt[...] = column(jnp.concatenate([wl_ref[0:1, :], wl_ref[1:2, :]], axis=1))
    gbt[...] = jnp.concatenate(
        [jnp.full((1, 128), gb_ref[t, k], F32) for t in range(2) for k in range(4)], axis=0
    )
    gate = jnp.concatenate([gate_ref[0], gate_ref[1]], axis=0)
    gate_low = gate.astype(BF16).astype(F32)
    gback[...] = jnp.concatenate([gate_low, gate_low, jnp.zeros((112, D), F32)], axis=0).T.astype(BF16)
    acc_gate[...] = jnp.zeros_like(acc_gate)
    acc_out[...] = jnp.zeros_like(acc_out)
    for hbuf in hbufs:
        for e in range(E):
            hbuf[e * HE + H : (e + 1) * HE, :] = jnp.ones((16, TF), BF16)
    acc_first[...] = jnp.zeros_like(acc_first)
    acc_second[...] = jnp.zeros_like(acc_second)
    acc_dlog[...] = jnp.zeros_like(acc_dlog)
    acc_lb[...] = jnp.zeros_like(acc_lb)
    acc_last[...] = jnp.zeros_like(acc_last)
    acc_b1[...] = jnp.zeros_like(acc_b1)
    acc_b2[...] = jnp.zeros_like(acc_b2)

    lane = lax.broadcasted_iota(jnp.int32, (128, 128), 1)

    def place(half, win, wout, bias):
        for e in range(E):
            at = pl.multiple_of(e * H + half * 128, 128)
            w = win[:, e * 128 : (e + 1) * 128]
            wf[pl.ds(at, 128), :] = w.T
            o = wout[:, e * H : (e + 1) * H]
            wot[pl.ds(e * H, H), pl.ds(pl.multiple_of(half * 128, 128), 128)] = o.T
            gain = column(bias[8 + e : 9 + e, :])
            pk[pl.ds(at, 128), :] = jnp.where(lane == 0, column(bias[e : e + 1, :]), gain)
            g2t[pl.ds(at, 128), :] = gain * 0.5
            b2t[pl.ds(at, 128), :] = column(bias[16 + e : 17 + e, :]) * 0.5

    place(mp, win_snd, wout_snd, bias_snd)
    for copy in st_copies:
        copy.wait()
    total, square, count = merge_stats([st_near[k] for k in range(2 * plan[0][1])])
    for level in range(1, n_levels):
        own = digits[level]
        st_lv[level, own] = jnp.concatenate([total, square, count, jnp.zeros((5, D), F32)], axis=0)
        copies = []
        for step in range(1, plan[level][1]):
            base = 2 * (len(near) + level * 3 + step - 1)
            copies.append(
                send(
                    st_lv.at[level, own], st_lv.at[level, own],
                    sem_st.at[base], sem_st.at[base + 1], peer(level, step),
                )
            )
        if level == 1:
            for copy in w_copies:
                copy.wait()
            place(other, win_rcv, wout_rcv, bias_rcv)
            keep = [
                pltpu.make_async_copy(win_snd, wb_hbm.at[mp], sem_f.at[0]),
                pltpu.make_async_copy(win_rcv, wb_hbm.at[other], sem_f.at[1]),
            ]
            for copy in keep:
                copy.start()
            means = []
            for e in range(E):
                w = wf[e * H : (e + 1) * H, :].astype(F32)
                means.append(jnp.sum(w, axis=0, keepdims=True) * (1.0 / H))
                shift = jnp.sum(pk[e * H : (e + 1) * H, 0:1], axis=0, keepdims=True) * (1.0 / H)
                for k in range(2):
                    at = slice(e * H + k * 128, e * H + (k + 1) * 128)
                    table = pk[at, :]
                    table = jnp.where(lane == 0, table - shift, table)
                    second = column(bout_ref[e : e + 1, k * 128 : (k + 1) * 128])
                    pk[at, :] = jnp.where(lane == 1, second, table)
            pad = [jnp.zeros((2, D), F32)]
            means = jnp.concatenate(means + pad, axis=0)
            means_high = means.astype(BF16).astype(F32)
            wf[E * H : E * H + 32, :] = jnp.concatenate(
                [gate_low, means_high, means - means_high, jnp.zeros((8, D), F32)], axis=0
            ).astype(BF16)
        for copy in copies:
            copy.wait()
        total, square, count = merge_stats([st_lv[level, k] for k in range(plan[level][1])])
    mu = total / count
    inv = lax.rsqrt(square / count + EPS)
    stat_ref[...] = jnp.concatenate([mu, inv, count, jnp.zeros((5, D), F32)], axis=0)

    def forward(i, side):
        abuf, hbuf = abufs[side], hbufs[side]
        r0 = pl.multiple_of(i * TF, TF)
        x_tile = xbuf[pl.ds(r0, TF), :].astype(F32)
        xn = ((x_tile - stat_ref[0:1, :]) * stat_ref[1:2, :]).astype(BF16)
        xbuf[pl.ds(r0, TF), :] = xn
        ext = nt(wf[E * H : E * H + 32, :], xn)
        logit_bufs[side][...] = ext[0:8] + wide(gbt[...], TF)
        means = ext[8:16] + ext[16:24]

        def product(e):
            abuf[e * H : (e + 1) * H, :] = nt(wf[e * H : (e + 1) * H, :], xn)

        def norm(e):
            squares = jnp.zeros((8, TF), F32)
            for at in range(e * H, (e + 1) * H, CH):
                c = (abuf[at : at + CH, :] - means[e : e + 1]) + pk[at : at + CH, 0:1]
                abuf[at : at + CH, :] = c
                squares = squares + fold8(c * c)
            r = lax.rsqrt(jnp.sum(squares, axis=0, keepdims=True) * (1.0 / H) + EPS)
            rbuf[e : e + 1, pl.ds(r0, TF)] = r
            for u in range(0, H, CH):
                at = e * H + u
                zhat = abuf[at : at + CH, :] * r
                zbuf[at : at + CH, pl.ds(r0, TF)] = zhat.astype(BF16)
                half = zhat * wide(g2t[at : at + CH, :], TF) + wide(b2t[at : at + CH, :], TF)
                p = 1.0 + jnp.tanh(half)
                h = half * p
                hbuf[e * HE + u : e * HE + u + CH, :] = h.astype(BF16)
                slope = (p + h * (2.0 - p)) * pk[at : at + CH, 2:3]
                sbuf[at : at + CH, pl.ds(r0, TF)] = slope.astype(BF16)

        def output(e):
            o = nn(wot[e * H : (e + 1) * H, :], hbuf[e * HE : e * HE + H, :])
            abuf[e * H : (e + 1) * H, :] = o + pk[e * H : (e + 1) * H, 1:2]

        product(0)
        product(1)
        yield
        for e in range(E):
            norm(e)
            if e + 2 < E:
                product(e + 2)
            output(e)
            yield

    def heads(i, side):
        abuf, hbuf = abufs[side], hbufs[side]
        r0 = pl.multiple_of(i * TF, TF)
        v0 = pl.multiple_of(mp * R + i * TF, 128)
        logits = logit_bufs[side][...]
        probs = []
        for t in range(2):
            part = logits[4 * t : 4 * t + 4]
            part = jnp.exp(part - jnp.max(part, axis=0, keepdims=True))
            part = part / jnp.sum(part, axis=0, keepdims=True)
            probs.append([part[k : k + 1] for k in range(4)])
        for at in range(0, H, CH):
            for t in range(2):
                mixed = None
                for k in range(4):
                    e = TASK_EXPERTS[t][k]
                    term = probs[t][k] * abuf[e * H + at : e * H + at + CH, :]
                    mixed = term if mixed is None else mixed + term
                mixb[t * H + at : t * H + at + CH, :] = mixed.astype(BF16)
        pres = [nn(w1t[t], mixb[t * H : (t + 1) * H, :]) for t in range(2)]
        yield
        slopes = []
        for t in range(2):
            half = pres[t] + wide(b1t[t * 128 : (t + 1) * 128, :], TF)
            p = 1.0 + jnp.tanh(half)
            u1 = half * p
            u1b[t * 128 : (t + 1) * 128, :] = u1.astype(BF16)
            slopes.append(p + u1 * (2.0 - p))
        pre = nn(w2f[...], u1b[...])
        yield
        half = pre + wide(b2tt[...], TF)
        p = 1.0 + jnp.tanh(half)
        u2 = half * p
        slope2 = p + u2 * (2.0 - p)
        wl = wide(wlt[...], TF)
        weighted = u2 * wl
        d_logits = []
        valid = v_ref[:, pl.ds(v0, TF)].astype(F32)
        for t in range(2):
            logit = jnp.sum(weighted[t * 64 : (t + 1) * 64], axis=0, keepdims=True) + bl_ref[t]
            pred = 0.5 + 0.5 * jnp.tanh(0.5 * logit)
            predbuf[t : t + 1, pl.ds(r0, TF)] = pred
            label = y_ref[t : t + 1, pl.ds(v0, TF)].astype(F32)
            d_logits.append(valid * (pred - label))
        d_logit = jnp.concatenate(
            [jnp.broadcast_to(d_logits[t], (64, TF)) for t in range(2)], axis=0
        )
        acc_last[...] += fold_lanes(u2 * d_logit)
        acc_lb[0:2] += fold_lanes(jnp.concatenate(d_logits, axis=0))
        d2 = (d_logit * 0.5) * (wl * slope2)
        acc_b2[...] += fold_lanes(d2)
        d2_low = d2.astype(BF16)
        d_u1 = nn(w2b[...], d2_low)
        acc_second[...] += nt(d2_low, u1b[...])
        yield
        for t in range(2):
            d1 = d_u1[t * 128 : (t + 1) * 128] * slopes[t]
            acc_b1[t * 128 : (t + 1) * 128] += fold_lanes(d1)
            d1_low = d1.astype(BF16)
            dmix[t * H : (t + 1) * H, :] = nn(w1n[t], d1_low)
            acc_first[t] += nt(mixb[t * H : (t + 1) * H, :], d1_low)
        yield
        dots = [[jnp.zeros((8, TF), F32) for _ in range(4)] for _ in range(2)]
        for at in range(0, H, CH):
            dm = [dmix[t * H + at : t * H + at + CH, :] for t in range(2)]
            grads = [None] * E
            for t in range(2):
                for k in range(4):
                    e = TASK_EXPERTS[t][k]
                    term = probs[t][k] * dm[t]
                    grads[e] = term if grads[e] is None else grads[e] + term
                    o = abuf[e * H + at : e * H + at + CH, :]
                    dots[t][k] = dots[t][k] + fold8(dm[t] * o)
            for e in range(E):
                dobuf[e * H + at : e * H + at + CH, pl.ds(r0, TF)] = grads[e].astype(BF16)
        rows = []
        for t in range(2):
            sums = [jnp.sum(dots[t][k], axis=0, keepdims=True) for k in range(4)]
            centre = sum(probs[t][k] * sums[k] for k in range(4))
            rows += [probs[t][k] * (sums[k] - centre) for k in range(4)]
        d_gate = jnp.concatenate(rows, axis=0)
        acc_dlog[...] += fold_lanes(d_gate)
        high = d_gate.astype(BF16).astype(F32)
        d_gate = jnp.concatenate([high, d_gate - high], axis=0).astype(BF16)
        dlogbuf[:, pl.ds(r0, TF)] = d_gate
        acc_gate[...] += nn(d_gate, xbuf[pl.ds(r0, TF), :])
        yield
        for e in range(E):
            at = pl.ds(e * HE, HE)
            acc_out[at, :] += nt(hbuf[at, :], dobuf[e * H : (e + 1) * H, pl.ds(r0, TF)])
        yield

    def together(*parts):
        parts = list(parts)
        while parts:
            for part in list(parts):
                if next(part, "end") == "end":
                    parts.remove(part)

    for copy in keep:
        copy.wait()
    n_f = R // TF
    together(forward(0, 0))

    def forward_pair(j, carry):
        together(heads(2 * j, 0), forward(2 * j + 1, 1))
        together(heads(2 * j + 1, 1), forward(2 * j + 2, 0))
        return carry

    lax.fori_loop(0, n_f // 2 - 1, forward_pair, 0)
    together(heads(n_f - 2, 0), forward(n_f - 1, 1))
    together(heads(n_f - 1, 1))

    pending = []
    pred_at = pl.ds(pl.multiple_of(mp * R, 128), R)
    pred_local = pltpu.make_async_copy(predbuf, pred_hbm.at[:, pred_at], sem_l.at[0])
    pred_local.start()
    pending.append(pred_local)
    pending.append(send(predbuf, pred_hbm.at[:, pred_at], sem_w.at[6], sem_w.at[7], (b, other)))

    flight = {}
    n_sems = 1 + 2 * sum(radix - 1 for _, radix, _, _ in plan)

    def source(c, rows, place_at):
        w = WIDTHS[c]
        at = sum(p[2] for p in plan[1:place_at])
        if c < E:
            return sbuf.at[pl.ds(c * H + at, rows), pl.ds(min(place_at, 1) * w, w)]
        if place_at:
            return sends_low.at[c - E, pl.ds(at, rows), :]
        return sends.at[c - E, pl.ds(0, rows), :]

    def level_sems(level):
        return 1 + 2 * sum(radix - 1 for _, radix, _, _ in plan[:level])

    def start_pair(c):
        src = source(c, H, 0)
        flight[c] = [send(src, mprecv[c], sem_s.at[c, 0], sem_r.at[c, 0], (b, other))]

    def start_level(c, level, value):
        stride, radix, rows, after = plan[level]
        out = source(c, rows, level)
        out[...] = value.astype(BF16)
        copies = []
        for step in range(1, radix):
            k = level_sems(level) + step - 1
            part = out
            if after != rows:
                to = lax.rem(digits[level] + step, radix)
                part = out.at[pl.ds(pl.multiple_of(to * after, 16), after), :]
            dst = lvrecv[c][level].at[step]
            copies.append(send(part, dst, sem_s.at[c, k], sem_r.at[c, k], peer(level, step)))
        flight[c] = copies
        if after != rows:
            mine = out[pl.ds(pl.multiple_of(digits[level] * after, 16), after), :]
        else:
            mine = out[...]
        lvrecv[c][level][0] = mine

    def finish_level(c, level):
        stride, radix, rows, after = plan[level]
        for copy in flight[c]:
            copy.wait()
        if after != rows:
            parts = [lvrecv[c][level][step].astype(F32) for step in range(radix)]
            return functools.reduce(lambda p, q: p + q, parts)
        total = None
        for k in range(radix):
            step = lax.rem(k - digits[level] + radix, radix)
            part = lvrecv[c][level][step].astype(F32)
            total = part if total is None else total + part
        return total

    def region(c, level):
        at = 0
        for k in range(level + 1):
            if plan[k][2] != plan[k][3]:
                at = at + digits[k] * plan[k][3]
        rows = plan[level][3] if level >= 0 else H
        if isinstance(at, int):
            return gout_hbm.at[c, pl.ds(at, rows), pl.ds(0, WIDTHS[c])]
        return gout_hbm.at[c, pl.ds(pl.multiple_of(at, 16), rows), pl.ds(0, WIDTHS[c])]

    split = [level for level in range(n_levels) if plan[level][2] != plan[level][3]]

    def start_result(c, value):
        rows = plan[-1][3]
        final = source(c, rows, n_levels)
        final[...] = value.astype(BF16)
        local = pltpu.make_async_copy(final, region(c, n_levels - 1), sem_l.at[1 + c])
        local.start()
        flight[c] = [local]
        if split:
            start_gather(c, split[-1], final)

    def start_gather(c, level, src):
        dst = region(c, level)
        for step in range(1, plan[level][1]):
            k = level_sems(level) + plan[level][1] - 1 + step - 1
            flight[c].append(send(src, dst, sem_s.at[c, k], sem_r.at[c, k], peer(level, step)))

    def chunk_steps(c):
        steps = []

        def from_pair():
            for copy in flight[c]:
                copy.wait()
            if c < E:
                value = hkeep[c % 2][...]
            elif c == TOWERS:
                value = source(c, H, 0)[...].astype(F32)
            else:
                value = half_out(c - TOWERS - 1, mp)
            start_level(c, 0, value + mprecv[c][...].astype(F32))

        steps.append(from_pair)
        for level in range(n_levels):

            def next_level(level=level):
                value = finish_level(c, level)
                if level + 1 < n_levels:
                    start_level(c, level + 1, value)
                else:
                    start_result(c, value)

            steps.append(next_level)
        for place_in in range(len(split) - 1, 0, -1):

            def gather(place_in=place_in):
                for copy in flight[c]:
                    copy.wait()
                flight[c] = []
                start_gather(c, split[place_in - 1], region(c, split[place_in] - 1))

            steps.append(gather)

        def finish():
            for copy in flight[c]:
                copy.wait()
            flight[c] = []

        steps.append(finish)
        return steps

    queue = []
    clock = [0]

    def start_steps(steps, spacing):
        queue.append([clock[0] + spacing, spacing, steps])

    def turn():
        clock[0] += 1
        for item in list(queue):
            if clock[0] >= item[0]:
                item[2].pop(0)()
                item[0] = clock[0] + item[1]
                if not item[2]:
                    queue.remove(item)

    def half_out(group, h):
        parts = []
        for e in range(3 * group, 3 * group + 3):
            a = acc_out[pl.ds(pl.multiple_of(e * HE + h * 128, 16), 128), :]
            parts.append(jnp.concatenate([a[:, 0:128], a[:, 128:256]], axis=0))
        return jnp.concatenate(parts, axis=1)

    def half_in(h):
        at = pl.ds(pl.multiple_of(h * 128, 128), 128)
        return jnp.concatenate([acc_in[0][at, :], acc_in[1][at, :]], axis=0)

    def pack_towers():
        src = source(TOWERS, H, 0)
        src[:, 0:128] = acc_first[0].astype(BF16)
        src[:, 128:256] = acc_first[1].astype(BF16)
        gates = acc_gate[0:8] + acc_gate[8:16]
        rest = [acc_second[0:64, 0:128], acc_second[64:128, 128:256]]
        rest += [gates[:, k * 128 : (k + 1) * 128] for k in range(4)]
        rest.append(jnp.zeros((H - 160, 128), F32))
        src[:, 256:384] = jnp.concatenate(rest, axis=0).astype(BF16)

    def launch(c, spacing=4):
        start_pair(c)
        start_steps(chunk_steps(c), spacing)

    pack_towers()
    launch(TOWERS)

    def launch_out(group):
        source(TOWERS + 1 + group, H, 0)[...] = half_out(group, other).astype(BF16)
        launch(TOWERS + 1 + group)

    s2row[...] = jnp.sum(
        (gate_low * (acc_gate[0:8] + acc_gate[8:16])), axis=0, keepdims=True
    )

    def backward_start(e, i):
        rows = slice(e * H, (e + 1) * H)
        for part in range(TB // SB):
            lanes = pl.ds(pl.multiple_of(i * TB + part * SB, SB), SB)
            dmix[part * H : (part + 1) * H, :] = nn(wot[rows, :], dobuf[rows, lanes])

    def backward_part(e, r0, part):
        at0 = e * H
        lanes = pl.ds(r0, SB)
        work = dmix.at[part * H : (part + 1) * H]
        r = rbuf[e : e + 1, lanes]
        m1 = jnp.zeros((8, SB), F32)
        m2 = jnp.zeros((8, SB), F32)
        for u in range(0, H, CH):
            at = at0 + u
            zhat = zbuf[at : at + CH, lanes].astype(F32)
            dzg = work[u : u + CH, :] * sbuf[at : at + CH, lanes].astype(F32)
            q = dzg * zhat
            acc_u[0][u : u + CH, :] += fold_lanes(dzg)
            acc_u[1][u : u + CH, :] += fold_lanes(q)
            work[u : u + CH, :] = dzg
            m1 = m1 + fold8(dzg)
            m2 = m2 + fold8(q)
        m1 = jnp.sum(m1, axis=0, keepdims=True) * (1.0 / H)
        m2 = jnp.sum(m2, axis=0, keepdims=True) * (1.0 / H)
        for u in range(0, H, CH):
            at = at0 + u
            zhat = zbuf[at : at + CH, lanes].astype(F32)
            da = r * (work[u : u + CH, :] - m1 - zhat * m2)
            acc_u[2][u : u + CH, :] += fold_lanes(da)
            zbuf[at : at + CH, lanes] = da.astype(BF16)

    n_b = R // TB

    def weight_part(e, i):
        r0 = pl.multiple_of(i * TB, TB)
        rows = slice(e * H, (e + 1) * H)
        grad = nn(zbuf[rows, pl.ds(r0, TB)], xbuf[pl.ds(r0, TB), :])
        acc_in[0][...] += grad[:, 0:256]
        acc_in[1][...] += grad[:, 256:512]

    def backward_tile(e, i):
        for part in range(TB // SB):
            backward_part(e, pl.multiple_of(i * TB + part * SB, SB), part)

    def clear_units():
        for part in acc_u:
            part[...] = jnp.zeros((H, 128), F32)

    def clear_weights():
        for part in acc_in:
            part[...] = jnp.zeros((H, 256), F32)

    def finish_units(e):
        for k in range(3):
            sums = lane_sums(acc_u[2 - k][...])
            v_mp[mp, k * 12 + 2 * e : k * 12 + 2 * e + 1, :] = sums[:, 0:128]
            v_mp[mp, k * 12 + 2 * e + 1 : k * 12 + 2 * e + 2, :] = sums[:, 128:256]
        bo = acc_out[e * HE + H : e * HE + H + 1, :]
        v_mp[mp, 36 + 2 * e : 37 + 2 * e, :] = bo[:, 0:128]
        v_mp[mp, 37 + 2 * e : 38 + 2 * e, :] = bo[:, 128:256]
        clear_units()

    def finish_expert(e):
        hkeep[e % 2][...] = half_in(mp)
        source(e, H, 0)[...] = half_in(other).astype(BF16)
        launch(e, 2 if e == E - 1 else 3 if e == E - 2 else 4)
        cross = jnp.zeros((8, D), F32)
        for u in range(0, H, CH):
            w = wf[e * H + u : e * H + u + CH, :].astype(F32)
            grad = jnp.concatenate([acc_in[0][u : u + CH, :], acc_in[1][u : u + CH, :]], axis=1)
            cross = cross + fold8(w * grad)
        s2row[...] += jnp.sum(cross, axis=0, keepdims=True)
        clear_weights()

    clear_weights()
    clear_units()
    for e in range(E):
        rows = slice(e * H, (e + 1) * H)
        wot[rows, :] = (wot[rows, :].T.astype(F32) * 0.5).astype(BF16)
    for e in range(E):

        def backward_step(i, carry, e=e):
            backward_start(e, i)
            weight_part(e, i - 1)
            backward_tile(e, i)
            return carry

        backward_start(e, 0)
        if e:
            weight_part(e - 1, n_b - 1)
        backward_tile(e, 0)
        if e:
            finish_expert(e - 1)
        if e == 2:
            back = []
            for k in range(2 * E):
                half, to = k % 2, 2048 + k * 128
                copy = pltpu.make_async_copy(
                    wb_hbm.at[half, :, (k // 2) * 128 : (k // 2 + 1) * 128],
                    sbuf.at[0:D, to : to + 128],
                    sem_f.at[k],
                )
                copy.start()
                back.append(copy)
        turn()
        if e == 0:
            launch_out(0)
        for k in range(3):
            first, last = 1 + k * (n_b - 1) // 3, 1 + (k + 1) * (n_b - 1) // 3
            lax.fori_loop(first, last, backward_step, 0)
            turn()
            if e == 0 and k == 1:
                launch_out(1)
        finish_units(e)
    weight_part(E - 1, n_b - 1)
    finish_expert(E - 1)
    for copy in back:
        copy.wait()
    wb = sbuf.at[0:D, 2048 : 2048 + E * H]
    for k in range(4):
        g2t[k * 128 : (k + 1) * 128, :] = column(stat_ref[1:2, k * 128 : (k + 1) * 128])

    for k in range(4):
        v_mp[mp, 48 + k : 49 + k, :] = s2row[:, k * 128 : (k + 1) * 128]
    v_mp[mp, 52:60, :] = acc_dlog[...]
    v_mp[mp, 60:61, :] = lane_sums(acc_last[...])
    v_mp[mp, 61:63, :] = acc_lb[0:2]
    b1_sums = lane_sums(acc_b1[...])
    v_mp[mp, 63:64, :] = b1_sums[:, 0:128]
    v_mp[mp, 64:65, :] = b1_sums[:, 128:256]
    v_mp[mp, 65:66, :] = lane_sums(acc_b2[...])
    v_mp[mp, 66:VR, :] = jnp.zeros((VR - 66, 128), F32)
    flight["v"] = [send(v_mp.at[mp], v_mp.at[mp], sem_v.at[0], sem_v.at[1], (b, other))]

    def small_level(level, total):
        own = digits[level]
        v_lv[level, own] = total
        flight["v"] = []
        for step in range(1, plan[level][1]):
            base = 2 + (level * 3 + step - 1) * 2
            flight["v"].append(
                send(
                    v_lv.at[level, own], v_lv.at[level, own],
                    sem_v.at[base], sem_v.at[base + 1], peer(level, step),
                )
            )

    def small_steps():
        steps = []

        def first():
            for copy in flight["v"]:
                copy.wait()
            small_level(0, v_mp[0] + v_mp[1])

        steps.append(first)
        for level in range(n_levels):

            def step(level=level):
                for copy in flight["v"]:
                    copy.wait()
                total = v_lv[level, 0]
                for k in range(1, plan[level][1]):
                    total = total + v_lv[level, k]
                if level + 1 < n_levels:
                    small_level(level + 1, total)
                    return
                vout_ref[...] = total
                row = jnp.concatenate([total[k : k + 1] for k in range(2 * E)], axis=1)
                row_high = row.astype(BF16).astype(F32)
                rows = jnp.concatenate(
                    [row_high, row - row_high, jnp.zeros((14, E * H), F32)], axis=0
                ).astype(BF16)
                s1 = nn(rows, wf[0 : E * H, :])
                gate_sum = jnp.sum(total[52:60], axis=1, keepdims=True)
                gate_part = jnp.sum(gate_low * gate_sum, axis=0, keepdims=True)
                stat_ref[3:4, :] = s1[0:1] + s1[1:2] + gate_part
                stat_ref[4:5, :] = jnp.concatenate([total[48 + k : 49 + k] for k in range(4)], axis=1)

            steps.append(step)
        return steps

    start_steps(small_steps(), 2)
    turn()

    def input_gradient(i):
        lanes = pl.ds(i * TB, TB)
        da = zbuf[:, lanes]
        dl = dlogbuf[:, lanes]
        for k, half in ((0, mp), (1, other)):
            at = pl.ds(pl.multiple_of(half * 256, 256), 256)
            grad = nn(wb[at, :], da) + nn(gback[at, 0:16], dl)
            grad = grad * wide(g2t[at, :], TB)
            dobuf[k * H : (k + 1) * H, lanes] = grad.astype(BF16)

    n_c = R // TB
    for part in range(4):
        for k in range(part * n_c // 4, (part + 1) * n_c // 4):
            input_gradient(k)
            turn()
        w = R // 4
        at = pl.ds(part * w, w)
        to = pl.ds(pl.multiple_of(mp * R + part * w, 128), w)
        local = pltpu.make_async_copy(dobuf.at[0:H, at], d_hbm.at[:, to], sem_l.at[1 + NC + part])
        local.start()
        pending.append(local)
        pending.append(
            send(dobuf.at[H : 2 * H, at], d_hbm.at[:, to], sem_d.at[part], sem_d.at[4 + part], (b, other))
        )
    while queue:
        turn()
    for copy in pending:
        copy.wait()


def final_kernel(
    tile, dt_ref, x_ref, v_ref, gain_ref, pred_ref, gout_ref, vout_ref, stat_ref,
    o_pred, o_feat, o_in, o_inb, o_gain, o_nb, o_out, o_outb, o_gate, o_gateb,
    o_w1, o_b1, o_w2, o_b2, o_wl, o_bl,
):
    mp = lax.axis_index("mp")
    half = pl.ds(pl.multiple_of(mp * 256, 256), 256)

    count = stat_ref[2:3, half]
    inv = stat_ref[1:2, half]
    slope = inv * inv * (stat_ref[4:5, half] / count)
    shift = inv * (stat_ref[3:4, half] / count) - stat_ref[0:1, half] * slope
    eye = jnp.where(
        lax.broadcasted_iota(jnp.int32, (256, 256), 0) == lax.broadcasted_iota(jnp.int32, (256, 256), 1), 1.0, 0.0
    ).astype(BF16)
    for at in range(0, tile, 256):
        rows = slice(at, at + 256)
        grad = nt(eye, dt_ref[:, rows])
        valid = nt(eye, jnp.broadcast_to(v_ref[:, rows].astype(F32), (128, 256)).astype(BF16))
        for c in range(2):
            cols = slice(c * 128, (c + 1) * 128)
            term = valid * (shift[:, cols] + x_ref[rows, cols].astype(F32) * slope[:, cols])
            o_feat[rows, cols] = grad[:, cols] - term

    @pl.when(pl.program_id(0) == 0)
    def _():
        scale = 1.0 / stat_ref[2:3, 0:128]
        one = scale[:, 0:1]
        o_pred[...] = pred_ref[...]
        for e in range(E):
            for k in range(4):
                g = gout_ref[e, (k // 2) * 128 : (k // 2 + 1) * 128, (k % 2) * 128 : (k % 2 + 1) * 128]
                o_in[e, k * 128 : (k + 1) * 128, :] = (g.astype(F32) * one).T
            for k in range(2):
                g = gout_ref[TOWERS + 1 + e // 3, k * 128 : (k + 1) * 128, (e % 3) * 128 : (e % 3 + 1) * 128]
                o_out[e, :, k * 128 : (k + 1) * 128] = g.astype(F32) * one
            for ref, base in ((o_inb, 0), (o_gain, 12), (o_nb, 24)):
                sums = vout_ref[pl.ds(base + 2 * e + mp, 1), :] * scale
                ref[e : e + 1, :] = sums / gain_ref[e : e + 1, :] if base else sums
            for k in range(2):
                o_outb[e : e + 1, k * 128 : (k + 1) * 128] = (
                    vout_ref[36 + 2 * e + k : 37 + 2 * e + k, :] * scale
                )
        o_w1[0] = gout_ref[TOWERS, :, 0:128].astype(F32) * one
        o_w1[1] = gout_ref[TOWERS, :, 128:256].astype(F32) * one
        g = gout_ref[TOWERS, 0:160, 256:384].astype(F32) * one
        o_w2[0] = g[0:64]
        o_w2[1] = g[64:128]
        for k in range(4):
            part = g[128 + 8 * k : 136 + 8 * k]
            o_gate[0, :, k * 128 : (k + 1) * 128] = part[0:4]
            o_gate[1, :, k * 128 : (k + 1) * 128] = part[4:8]
        gate_bias = jnp.sum(vout_ref[52:60, :], axis=1, keepdims=True) * scale
        table = jnp.concatenate([gate_bias, jnp.zeros((120, 128), F32)], axis=0).T
        o_gateb[0:1, :] = table[0:1, 0:4]
        o_gateb[1:2, :] = table[0:1, 4:8]
        last = vout_ref[60:61, :] * scale
        o_wl[0:1, :] = last[:, 0:64]
        o_wl[1:2, :] = last[:, 64:128]
        o_bl[...] = jnp.sum(vout_ref[61:63, :], axis=1, keepdims=True) * scale
        o_b1[...] = vout_ref[63:65, :] * scale
        b2 = vout_ref[65:66, :] * scale
        o_b2[0:1, :] = b2[:, 0:64]
        o_b2[1:2, :] = b2[:, 64:128]


def on_device(
    features, validity, labels, expert_in, expert_in_bias, norm_gain, norm_bias, expert_out,
    expert_out_bias, gate_weight, gate_bias, tower_first, tower_first_bias, tower_second,
    tower_second_bias, tower_last, tower_last_bias,
):
    rows = features.shape[0]
    R = rows // 2
    n_batch = lax.axis_size("batch")
    plan = plan_of(n_batch)
    n_levels = len(plan)
    n_peers = sum(radix - 1 for _, radix, _, _ in plan)
    n_sems = 1 + 2 * n_peers
    v_row = validity.reshape(1, rows)
    y_rows = labels.T
    vm = pl.BlockSpec(memory_space=pltpu.VMEM)
    sm = pl.BlockSpec(memory_space=pltpu.SMEM)
    hb = pl.BlockSpec(memory_space=pl.ANY)
    dma = pltpu.SemaphoreType.DMA

    def scr(*shape, dtype=F32):
        return pltpu.VMEM(shape, dtype)

    low_rows = sum(p[2] for p in plan[1:]) + plan[-1][3]
    scratch = [
        scr(R, D, dtype=BF16), scr(E * H, R, dtype=BF16), scr(E * H, R, dtype=BF16),
        scr(E * H, R, dtype=BF16), scr(8, R), scr(16, R, dtype=BF16), scr(2, R),
        scr(E * H + 32, D, dtype=BF16), scr(D, 128, dtype=BF16),
        scr(E * H, H, dtype=BF16), scr(E * H, 128), scr(E * H, 128), scr(E * H, 128),
        scr(2, 128, H, dtype=BF16), scr(2, H, 128, dtype=BF16), scr(128, H, dtype=BF16),
        scr(H, 128, dtype=BF16), scr(H, 128), scr(128, 128), scr(128, 128), scr(8, 128),
        [scr(E * H, TF)] * 2, [scr(E * HE, TF, dtype=BF16)] * 2, [scr(8, TF)] * 2,
        scr(2 * H, TF, dtype=BF16), scr(H, TF, dtype=BF16), scr(2 * H, TF),
        scr(E * HE, H), scr(16, D), scr(2, H, 128), scr(128, H),
        scr(8, 128), scr(8, 128), scr(128, 128), scr(128, 128), scr(H, 128), scr(1, D),
        scr(24, 128), scr(24, 128),
        scr(8, 8, D), scr(n_levels, 4, 8, D), scr(2, VR, 128), scr(n_levels, 4, VR, 128),
        scr(3, H, 384, dtype=BF16), scr(3, low_rows, 384, dtype=BF16),
        [scr(H, w, dtype=BF16) for w in WIDTHS],
        [[scr(radix, after, w, dtype=BF16) for _, radix, _, after in plan] for w in WIDTHS],
        dma((8,)), dma((8,)), dma((14 + 6 * n_levels,)), dma((2 + 6 * n_levels,)),
        dma((NC, n_sems)), dma((NC, n_sems)), dma((5 + NC,)), dma((8,)), dma((3 * E,)),
    ]
    flops = 2 * R * (6 * D * E * H // 2 + 3 * E * H * H)
    d_half, preds, gsum, vsum, stats, _ = pl.pallas_call(
        functools.partial(main_kernel, plan, R),
        out_shape=(
            jax.ShapeDtypeStruct((256, rows), BF16),
            jax.ShapeDtypeStruct((2, rows), F32),
            jax.ShapeDtypeStruct((NC, H, 384), BF16),
            jax.ShapeDtypeStruct((VR, 128), F32),
            jax.ShapeDtypeStruct((8, D), F32),
            jax.ShapeDtypeStruct((2, D, E * 128), BF16),
        ),
        in_specs=[hb] + [vm] * 2 + [hb] * 2 + [vm] * 5 + [sm] + [vm] * 5 + [sm],
        out_specs=(hb, hb, hb, vm, vm, hb),
        scratch_shapes=scratch,
        compiler_params=pltpu.CompilerParams(
            collective_id=0, has_side_effects=True, vmem_limit_bytes=64 * 2**20 - 65536
        ),
        cost_estimate=pl.CostEstimate(flops=flops, bytes_accessed=20 * 2**20, transcendentals=0),
        name="layer",
    )(
        features, v_row, y_rows, expert_in, expert_out, expert_in_bias, norm_gain, norm_bias,
        expert_out_bias, jnp.swapaxes(gate_weight, 1, 2), gate_bias, tower_first, tower_first_bias,
        jnp.swapaxes(tower_second, 1, 2), tower_second_bias, tower_last, tower_last_bias,
    )

    tile = 4096
    whole = lambda *shape: pl.BlockSpec(shape, lambda i: (0,) * len(shape))
    half_index = lambda i: (i, lax.axis_index("mp"))
    out_shapes = [
        (2, rows), (rows, 256), (E, D, 128), (E, 128), (E, 128), (E, 128), (E, 128, H), (E, H),
        (2, 4, D), (2, 4), (2, H, 128), (2, 128), (2, 64, 128), (2, 64), (2, 64), (2, 128),
    ]
    out_specs = [whole(*shape) for shape in out_shapes]
    out_specs[1] = pl.BlockSpec((tile, 256), lambda i: (i, 0))
    outs = pl.pallas_call(
        functools.partial(final_kernel, tile),
        grid=(rows // tile,),
        out_shape=[jax.ShapeDtypeStruct(shape, F32) for shape in out_shapes],
        in_specs=[
            pl.BlockSpec((256, tile), lambda i: (0, i)),
            pl.BlockSpec((tile, 256), half_index),
            pl.BlockSpec((1, tile), lambda i: (0, i)),
            whole(E, 128), whole(2, rows), whole(NC, H, 384), whole(VR, 128), whole(8, D),
        ],
        out_specs=out_specs,
        compiler_params=pltpu.CompilerParams(vmem_limit_bytes=64 * 2**20 - 65536),
        cost_estimate=pl.CostEstimate(
            flops=rows * 256 * 8, bytes_accessed=rows * 256 * 8, transcendentals=0
        ),
        name="finish",
    )(d_half, features, v_row, norm_gain, preds, gsum, vsum, stats)
    outs = list(outs)
    outs[0] = outs[0].T
    outs[8] = jnp.swapaxes(outs[8], 1, 2)
    outs[12] = jnp.swapaxes(outs[12], 1, 2)
    outs[15] = outs[15][:, 0]
    return tuple(outs)


def solution(mesh):
    in_specs = (
        P("batch", None), P("batch"), P("batch", None), P(None, None, "mp"), P(None, "mp"),
        P(None, "mp"), P(None, "mp"), P(None, "mp", None), P(), P(), P(), P(), P(), P(), P(), P(), P(),
    )
    out_specs = (
        P("batch", None), P("batch", "mp"), P(None, None, "mp"), P(None, "mp"), P(None, "mp"),
        P(None, "mp"), P(None, "mp", None), P(), P(), P(), P(), P(), P(), P(), P(), P(),
    )
    return jax.shard_map(
        on_device, mesh=mesh, in_specs=in_specs, out_specs=out_specs, check_vma=False
    )
```

profile of v0, /device:TPU:0, one launch (start us, length us, event | category | flops | bytes accessed | tf_op | source)
XLA Modules:
  0.0 135.0 jit_solution(15250989926140571432)
XLA Ops:
  0.7 123.8 %layer.1 = (bf16[256,8192]{1,0:T(8,128)(2,1)}, f32[2,8192]{1,0:T(2,128)}, bf16[9,256,384]{2,1,0:T(8,128)(2,1)}, f32[72,128]{1,0:T(8,128)}, f32[8,512]{1,0:T(8,128)}, /*index=5*/bf16[2,512,768]{2,1,0:T(8,128)(2,1)}) custom-call(bf16[8192,512]{1,0:T(8,128)(2,1)} %x_ref.1, s32[1,8192]{1,0:T(1,128)} %bitcast.7, s32[2,8192]{1,0:T(2,128)} %bitcast.9, ...), custom_call_target="tpu_custom_call" | custom-call | flops 28991029248 | bytes 20971520 | tf_op jit(solution)/shard_map/layer/pallas_call | solution.py:993
  124.5 9.0 %finish.1 = (f32[2,8192]{1,0:T(2,128)}, f32[8192,256]{1,0:T(8,128)}, f32[6,512,128]{2,1,0:T(8,128)}, f32[6,128]{1,0:T(8,128)}, f32[6,128]{1,0:T(8,128)}, /*index...) custom-call(bf16[256,8192]{1,0:T(8,128)(2,1)} %get-tuple-element.37., ...), custom_call_target="tpu_custom_call" | custom-call | flops 16777216 | bytes 16777216 | tf_op jit(solution)/shard_map/finish/pallas_call | solution.py:1026
  133.5 1.3 slice_reduce_fusion
where the time goes:
time: 137 us; the launch traced here: 135 us
  Pallas kernels  133 us (97%)
    pallas_call x1, Pallas kernels, on_device(): pl.pallas_call(functools.partial(main_kernel, plan, R), out_shape=(jax.Sh...  124 us
    pallas_call x1, Pallas kernels, on_device(): pl.pallas_call(functools.partial(final_kernel, tile), grid=(rows // tile,...  9.04 us

commit v1 on v0

--- a/solution.py
+++ b/solution.py
@@ -650,7 +650,7 @@
         rest.append(jnp.zeros((H - 160, 128), F32))
         src[:, 256:384] = jnp.concatenate(rest, axis=0).astype(BF16)
 
-    def launch(c, spacing=4):
+    def launch(c, spacing=3):
         start_pair(c)
         start_steps(chunk_steps(c), spacing)
 
@@ -731,7 +731,7 @@
     def finish_expert(e):
         hkeep[e % 2][...] = half_in(mp)
         source(e, H, 0)[...] = half_in(other).astype(BF16)
-        launch(e, 2 if e == E - 1 else 3 if e == E - 2 else 4)
+        launch(e, 2 if e >= E - 2 else 3)
         cross = jnp.zeros((8, D), F32)
         for u in range(0, H, CH):
             w = wf[e * H + u : e * H + u + CH, :].astype(F32)
@@ -773,8 +773,8 @@
         turn()
         if e == 0:
             launch_out(0)
-        for k in range(3):
-            first, last = 1 + k * (n_b - 1) // 3, 1 + (k + 1) * (n_b - 1) // 3
+        for k in range(2):
+            first, last = 1 + k * (n_b - 1) // 2, 1 + (k + 1) * (n_b - 1) // 2
             lax.fori_loop(first, last, backward_step, 0)
             turn()
             if e == 0 and k == 1:
@@ -896,14 +896,19 @@
     eye = jnp.where(
         lax.broadcasted_iota(jnp.int32, (256, 256), 0) == lax.broadcasted_iota(jnp.int32, (256, 256), 1), 1.0, 0.0
     ).astype(BF16)
-    for at in range(0, tile, 256):
-        rows = slice(at, at + 256)
-        grad = nt(eye, dt_ref[:, rows])
-        valid = nt(eye, jnp.broadcast_to(v_ref[:, rows].astype(F32), (128, 256)).astype(BF16))
-        for c in range(2):
-            cols = slice(c * 128, (c + 1) * 128)
-            term = valid * (shift[:, cols] + x_ref[rows, cols].astype(F32) * slope[:, cols])
-            o_feat[rows, cols] = grad[:, cols] - term
+
+    def block(i, carry):
+        for part in range(2):
+            rows = pl.ds(pl.multiple_of(i * 512 + part * 256, 256), 256)
+            grad = nt(eye, dt_ref[:, rows])
+            valid = nt(eye, jnp.broadcast_to(v_ref[:, rows].astype(F32), (128, 256)).astype(BF16))
+            for c in range(2):
+                cols = slice(c * 128, (c + 1) * 128)
+                term = valid * (shift[:, cols] + x_ref[rows, cols].astype(F32) * slope[:, cols])
+                o_feat[rows, cols] = grad[:, cols] - term
+        return carry
+
+    lax.fori_loop(0, tile // 512, block, 0)
 
     @pl.when(pl.program_id(0) == 0)
     def _():
@@ -940,7 +945,8 @@
         last = vout_ref[60:61, :] * scale
         o_wl[0:1, :] = last[:, 0:64]
         o_wl[1:2, :] = last[:, 64:128]
-        o_bl[...] = jnp.sum(vout_ref[61:63, :], axis=1, keepdims=True) * scale
+        table = jnp.sum(vout_ref[61:63, :], axis=1, keepdims=True) * scale
+        o_bl[...] = jnp.concatenate([table, jnp.zeros((126, 128), F32)], axis=0).T[0:1, 0:2]
         o_b1[...] = vout_ref[63:65, :] * scale
         b2 = vout_ref[65:66, :] * scale
         o_b2[0:1, :] = b2[:, 0:64]
@@ -1019,7 +1025,7 @@
     half_index = lambda i: (i, lax.axis_index("mp"))
     out_shapes = [
         (2, rows), (rows, 256), (E, D, 128), (E, 128), (E, 128), (E, 128), (E, 128, H), (E, H),
-        (2, 4, D), (2, 4), (2, H, 128), (2, 128), (2, 64, 128), (2, 64), (2, 64), (2, 128),
+        (2, 4, D), (2, 4), (2, H, 128), (2, 128), (2, 64, 128), (2, 64), (2, 64), (1, 2),
     ]
     out_specs = [whole(*shape) for shape in out_shapes]
     out_specs[1] = pl.BlockSpec((tile, 256), lambda i: (i, 0))
@@ -1044,7 +1050,7 @@
     outs[0] = outs[0].T
     outs[8] = jnp.swapaxes(outs[8], 1, 2)
     outs[12] = jnp.swapaxes(outs[12], 1, 2)
-    outs[15] = outs[15][:, 0]
+    outs[15] = outs[15].reshape(2)
     return tuple(outs)
 
 

time: 137 us -> 123 us (0.90); the launches traced: 135 us -> 123 us
  Pallas kernels: 133 us -> 122 us
    pallas_call x1, Pallas kernels: 124 us -> 111 us  [on_device(): pl.pallas_call(functools.partial(main_kernel, plan, R), out_shape=(jax.Sh...]
    pallas_call x1, Pallas kernels: 9.04 us -> 11.7 us  [on_device(): pl.pallas_call(functools.partial(final_kernel, tile), grid=(rows // tile,...]
where the time goes in v1:
time: 123 us
  Pallas kernels  122 us (99%)
    pallas_call x1, Pallas kernels, on_device(): pl.pallas_call(functools.partial(main_kernel, plan, R), out_shape=(jax.Sh...  111 us
    pallas_call x1, Pallas kernels, on_device(): pl.pallas_call(functools.partial(final_kernel, tile), grid=(rows // tile,...  11.7 us

profile of v1, /device:TPU:0, one launch (start us, length us, event | category | flops | bytes accessed | tf_op | source)
XLA Modules:
  0.0 123.0 jit_solution(15052057746532740789)
XLA Ops:
  0.7 110.5 %layer.1 = (bf16[256,8192]{1,0:T(8,128)(2,1)}, f32[2,8192]{1,0:T(2,128)}, bf16[9,256,384]{2,1,0:T(8,128)(2,1)}, f32[72,128]{1,0:T(8,128)}, f32[8,512]{1,0:T(8,128)}, /*index=5*/bf16[2,512,768]{2,1,0:T(8,128)(2,1)}) custom-call(bf16[8192,512]{1,0:T(8,128)(2,1)} %x_ref.1, s32[1,8192]{1,0:T(1,128)} %bitcast.8, s32[2,8192]{1,0:T(2,128)} %bitcast.10, ...), custom_call_target="tpu_custom_call" | custom-call | flops 28991029248 | bytes 20971520 | tf_op jit(solution)/shard_map/layer/pallas_call | solution.py:999
  111.2 11.7 %finish.1 = (f32[2,8192]{1,0:T(2,128)}, f32[8192,256]{1,0:T(8,128)}, f32[6,512,128]{2,1,0:T(8,128)}, f32[6,128]{1,0:T(8,128)}, f32[6,128]{1,0:T(8,128)}, /*index...) custom-call(bf16[256,8192]{1,0:T(8,128)(2,1)} %get-tuple-element.37., ...), custom_call_target="tpu_custom_call" | custom-call | flops 16777216 | bytes 16777216 | tf_op jit(solution)/shard_map/finish/pallas_call | solution.py:1032
